TPU v7x, 128 devices: a whole 4x4x4 slice. The times are simulated.
128 devices in a mesh: ctx: 32 (over x, z, core), head: 4 (over y).
Axes of the slice: x: 4, y: 4, z: 4, core: 2. Of those that a mesh axis runs over, the one named last changes fastest.
Arguments:
- queries: bfloat16 [16384, 2048], P(('ctx', 'head')), may hold values from -240 to 240
- keys_in: bfloat16 [16384, 2048], P(('ctx', 'head')), may hold values from -8 to 8
- values: bfloat16 [16384, 2048], P(('ctx', 'head')), may hold values from -6 to 6
- out_grad: bfloat16 [16384, 2048], P(('ctx', 'head')), may hold values from -6 to 6
- doc_lengths: int32 [15], replicated, may hold values from 1 to 2048, 16384 in all
Outputs:
- attended: bfloat16 [16384, 2048], P(('ctx', 'head'))
- query_grad: bfloat16 [16384, 2048], P(('ctx', 'head'))
- key_grad: bfloat16 [16384, 2048], P(('ctx', 'head'))
- value_grad: bfloat16 [16384, 2048], P(('ctx', 'head'))
Inputs may be any that keep to these rules, and one draw needn't show every extreme that they name: `doc_lengths`: each document has 1 to 2048 tokens, the longest exactly 2048; the lengths sum to 16384.
All inputs are finite; a program needn't handle non-finite values.
Results may differ from a plain program's by a relative error of at most 0.035.
Values may be sent and summed in bfloat16 or wider, within the bound.
A program may use at most 192 MiB of HBM per device.

v0:
```python
import functools

import jax
import jax.numpy as jnp
from jax import lax
from jax.experimental import pallas as pl
from jax.experimental.pallas import tpu as pltpu
from jax.sharding import PartitionSpec as P

HEAD_DIM = 128
NDOCS = 15
GROUP = 2048
PIECE = 128
PIECES = GROUP // PIECE
QT = 256
KT = 512
UNIT = 256
WINDOW = 3 * GROUP
PADDED = WINDOW + KT
SPAN = 9 * KT
TOKENS = 16384
MASK = 1024.0
SCALE = HEAD_DIM ** (-0.5)
LOG2E = 1.4426950408889634
MESH = pl.DeviceIdType.MESH
BF = jnp.bfloat16
F32 = jnp.float32


def place():
    ctx = lax.axis_index("ctx")
    y = lax.axis_index("head")
    x = ctx // 8
    z = (ctx // 2) % 4
    core = ctx % 2
    return x, z, core, y


def ctx_of(x, z, core):
    return (x * 4 + z) * 2 + core


def x_partner(x, core):
    return jnp.where(core == 0, (x + 3) % 4, (x + 1) % 4)


def gather_kernel(q_in, k_in, v_in, g_in, q_out, g_out, k_out, v_out, send, recv, hsend, hrecv):
    x, z, core, y = place()
    my_slot = ((2 * z + core) % 4) * 4 + y
    half = z // 2
    sibling = {"ctx": ctx_of(x, z, 1 - core), "head": y}
    beside = {"ctx": ctx_of(x_partner(x, core), z, 1 - core), "head": y}
    barrier = pltpu.get_barrier_semaphore()

    def is_self(zz, cc, yy):
        return (zz == z) & (cc == core) & (yy == y)

    def greet(s, c):
        zz = 2 * core + s // 8
        cc = (s // 4) % 2
        yy = s % 4

        @pl.when(jnp.logical_not(is_self(zz, cc, yy)))
        def _():
            pl.semaphore_signal(
                barrier, inc=1, device_id={"ctx": ctx_of(x, zz, cc), "head": yy}, device_id_type=MESH
            )

        return c

    lax.fori_loop(0, PIECES, greet, 0)
    pl.semaphore_signal(barrier, inc=1, device_id=sibling, device_id_type=MESH)
    pl.semaphore_signal(barrier, inc=1, device_id=beside, device_id_type=MESH)
    pl.semaphore_wait(barrier, jnp.where(half == core, PIECES - 1, PIECES) + 2)

    arrays = ((0, k_in, k_out), (1, v_in, v_out), (2, q_in, q_out), (3, g_in, g_out))

    def target(out, a):
        return out.at[1] if a < 2 else out

    def remote(a, src, out, step):
        zz = (z + step // 4) % 4
        yy = (y + step % 4) % 4
        head = zz * 4 + yy
        return (
            zz,
            yy,
            src.at[:, pl.ds(pl.multiple_of(head * HEAD_DIM, HEAD_DIM), HEAD_DIM)],
            target(out, a).at[pl.ds(pl.multiple_of(my_slot * PIECE, PIECE), PIECE), :],
        )

    def remote_copy(a, src, out, step):
        zz, yy, s_ref, d_ref = remote(a, src, out, step)
        return pltpu.make_async_remote_copy(
            src_ref=s_ref,
            dst_ref=d_ref,
            send_sem=send.at[a, step],
            recv_sem=recv.at[a, my_slot],
            device_id={"ctx": ctx_of(x, zz, half), "head": yy},
            device_id_type=MESH,
        )

    for a, src, out in arrays:

        @pl.when(half == core)
        def _():
            _, _, s_ref, d_ref = remote(a, src, out, 0)
            pltpu.make_async_copy(s_ref, d_ref, recv.at[a, my_slot]).start()

        @pl.when(half != core)
        def _():
            remote_copy(a, src, out, 0).start()

        def start(step, c):
            remote_copy(a, src, out, step).start()
            return c

        lax.fori_loop(1, PIECES, start, 0)

    def wait_all(a, out):
        def wait(s, c):
            piece = target(out, a).at[pl.ds(pl.multiple_of(s * PIECE, PIECE), PIECE), :]
            pltpu.make_async_copy(piece, piece, recv.at[a, s]).wait()
            return c

        lax.fori_loop(0, PIECES, wait, 0)

    halos = []
    for a, src, out in arrays[:2]:
        wait_all(a, out)
        sib = pltpu.make_async_remote_copy(
            src_ref=out.at[1],
            dst_ref=out.at[2 * core],
            send_sem=hsend.at[a, 0],
            recv_sem=hrecv.at[a, 0],
            device_id=sibling,
            device_id_type=MESH,
        )
        far = pltpu.make_async_remote_copy(
            src_ref=out.at[1],
            dst_ref=out.at[2 * (1 - core)],
            send_sem=hsend.at[a, 1],
            recv_sem=hrecv.at[a, 1],
            device_id=beside,
            device_id_type=MESH,
        )
        far.start()
        sib.start()
        halos += [sib, far]
    for a, src, out in arrays[2:]:
        wait_all(a, out)
    for copy in halos:
        copy.wait()
    for a, src, out in arrays:

        @pl.when(half != core)
        def _():
            remote_copy(a, src, out, 0).wait_send()

        def wait_sent(step, c):
            remote_copy(a, src, out, step).wait_send()
            return c

        lax.fori_loop(1, PIECES, wait_sent, 0)


def gather(q, k, v, g):
    any_spec = pl.BlockSpec(memory_space=pl.ANY)
    own = jax.ShapeDtypeStruct((GROUP, HEAD_DIM), BF)
    window = jax.ShapeDtypeStruct((3, GROUP, HEAD_DIM), BF)
    return pl.pallas_call(
        gather_kernel,
        out_shape=(own, own, window, window),
        in_specs=[any_spec] * 4,
        out_specs=(any_spec,) * 4,
        scratch_shapes=[
            pltpu.SemaphoreType.DMA((4, PIECES)),
            pltpu.SemaphoreType.DMA((4, PIECES)),
            pltpu.SemaphoreType.DMA((2, 2)),
            pltpu.SemaphoreType.DMA((2, 2)),
        ],
        compiler_params=pltpu.CompilerParams(collective_id=0, has_side_effects=True),
        name="to_heads",
    )(q, k, v, g)


def dot_nt(a, b):
    return lax.dot_general(a, b, (((1,), (1,)), ((), ())), preferred_element_type=F32)


def dot_nn(a, b):
    return lax.dot_general(a, b, (((1,), (0,)), ((), ())), preferred_element_type=F32)


def attend_kernel(
    lens, q_ref, g_ref, kw, vw, att_ref, dq_ref, own_ref, side_ref,
    ke, ve, s_scr, p_scr, o_acc, dq_acc, dk_acc, dv_acc,
):
    ctx = lax.axis_index("ctx")
    group = (ctx // 8) * 2 + ctx % 2
    base = (group - 1) * GROUP
    lane = lax.broadcasted_iota(jnp.int32, (1, 128), 1)
    starts = jnp.full((1, 128), 1 << 30, jnp.int32)
    ends = jnp.full((1, 128), 1 << 30, jnp.int32)
    bounds = [jnp.int32(0)]
    for j in range(NDOCS):
        starts = jnp.where(lane == j, bounds[-1], starts)
        bounds.append(bounds[-1] + lens[j])
        ends = jnp.where(lane == j, bounds[-1], ends)
    starts = jnp.where(lane == 127, TOKENS, jnp.where(lane == 126, -(1 << 30), starts))
    ends = jnp.where(lane == 126, 0, ends)
    row = lax.broadcasted_iota(jnp.int32, (QT, 128), 0)

    def in_doc(first):
        pos = first + row
        return (pos >= starts) & (pos < ends)

    ones = jnp.ones((QT, 128), BF)

    def build(b, c):
        rows = pl.ds(pl.multiple_of(b * QT, QT), QT)
        flag = jnp.where(in_doc(base + b * QT), -MASK, 0.0).astype(BF)
        ke[rows, :] = jnp.concatenate([kw[rows, :], flag], axis=1)
        ve[rows, :] = jnp.concatenate([vw[rows, :], ones], axis=1)
        return c

    lax.fori_loop(0, WINDOW // QT, build, 0)
    for b in range(WINDOW // QT, PADDED // QT):
        rows = pl.ds(b * QT, QT)
        flag = jnp.where(in_doc(base + b * QT), -MASK, 0.0).astype(BF)
        ke[rows, :] = jnp.concatenate([jnp.zeros((QT, 128), BF), flag], axis=1)
        ve[rows, :] = jnp.zeros((QT, 256), BF)
    dk_acc[...] = jnp.zeros_like(dk_acc)
    dv_acc[...] = jnp.zeros_like(dv_acc)

    lane_tile = lax.broadcasted_iota(jnp.int32, (QT, 128), 1)

    def query_tile(i, c):
        rows = pl.ds(pl.multiple_of(i * QT, QT), QT)
        r0 = group * GROUP + i * QT
        lo = jnp.int32(0)
        hi = jnp.int32(TOKENS)
        for e in bounds[1:]:
            lo = jnp.where(e <= r0, jnp.maximum(lo, e), lo)
            hi = jnp.where(e > r0 + (QT - 1), jnp.minimum(hi, e), hi)
        first = (lo - base) // UNIT
        steps = (hi - base - first * UNIT + (KT - 1)) // KT

        q = q_ref[rows, :]
        g = g_ref[rows, :]
        qe = jnp.concatenate([q, jnp.where(in_doc(r0), 0.0, MASK).astype(BF)], axis=1)

        def krows(t):
            return pl.ds(pl.multiple_of(first * UNIT + t * KT, UNIT), KT)

        def score_step(t, peak):
            s = dot_nt(qe, ke[krows(t), :])
            s_scr[t] = s
            for j in range(KT // 128):
                peak = jnp.maximum(peak, s[:, j * 128:(j + 1) * 128])
            return peak

        peak = lax.fori_loop(0, steps, score_step, jnp.full((QT, 128), -3e38, F32))
        peak = jnp.max(peak, axis=1, keepdims=True)

        o_acc[...] = jnp.zeros_like(o_acc)

        def prob_step(t, c):
            p = jnp.exp2((s_scr[t] - peak) * (SCALE * LOG2E)).astype(BF)
            p_scr[t] = p
            o_acc[...] += dot_nn(p, ve[krows(t), :])
            return c

        lax.fori_loop(0, steps, prob_step, 0)
        inv = 1.0 / o_acc[:, 128:]
        att = (o_acc[:, :128] * inv).astype(BF)
        att_ref[rows, :] = att
        g32 = g.astype(F32)
        neg = -jnp.sum(g32 * att.astype(F32), axis=1, keepdims=True)
        n0 = neg.astype(BF).astype(F32)
        n1 = (neg - n0).astype(BF).astype(F32)
        n2 = neg - n0 - n1
        extra = jnp.where(
            lane_tile == 0, n0, jnp.where(lane_tile == 1, n1, jnp.where(lane_tile == 2, n2, 0.0))
        ).astype(BF)
        ge = jnp.concatenate([g, extra], axis=1)
        gt = (g32 * inv).T.astype(BF)
        qt = (q.astype(F32) * (inv * SCALE)).T.astype(BF)
        dq_acc[...] = jnp.zeros_like(dq_acc)

        def grad_step(t, c):
            keys = krows(t)
            p = p_scr[t]
            dp = dot_nt(ge, ve[keys, :])
            ds = (p.astype(F32) * dp).astype(BF)
            dq_acc[...] += dot_nn(ds, ke[keys, :128])
            dk_acc[:, keys] += dot_nn(qt, ds)
            dv_acc[:, keys] += dot_nn(gt, p)
            return c

        lax.fori_loop(0, steps, grad_step, 0)
        dq_ref[rows, :] = (dq_acc[...] * (inv * SCALE)).astype(BF)
        return c

    lax.fori_loop(0, GROUP // QT, query_tile, 0)
    for a, acc in ((0, dk_acc), (1, dv_acc)):
        own_ref[a] = acc[:, GROUP:2 * GROUP]
        side_ref[a, 0] = acc[:, :GROUP].astype(BF)
        side_ref[a, 1] = acc[:, 2 * GROUP:3 * GROUP].astype(BF)


def attend(lens, q, g, kw, vw):
    vmem = pl.BlockSpec(memory_space=pltpu.VMEM)
    own = jax.ShapeDtypeStruct((GROUP, HEAD_DIM), BF)
    return pl.pallas_call(
        attend_kernel,
        out_shape=(
            own,
            own,
            jax.ShapeDtypeStruct((2, HEAD_DIM, GROUP), F32),
            jax.ShapeDtypeStruct((2, 2, HEAD_DIM, GROUP), BF),
        ),
        in_specs=[pl.BlockSpec(memory_space=pltpu.SMEM)] + [vmem] * 4,
        out_specs=(vmem,) * 4,
        scratch_shapes=[
            pltpu.VMEM((PADDED, 256), BF),
            pltpu.VMEM((PADDED, 256), BF),
            pltpu.VMEM((SPAN // KT, QT, KT), F32),
            pltpu.VMEM((SPAN // KT, QT, KT), BF),
            pltpu.VMEM((QT, 256), F32),
            pltpu.VMEM((QT, 128), F32),
            pltpu.VMEM((128, PADDED), F32),
            pltpu.VMEM((128, PADDED), F32),
        ],
        compiler_params=pltpu.CompilerParams(vmem_limit_bytes=56 * 1024 * 1024),
        name="attend",
    )(lens, q, g, kw.reshape(WINDOW, HEAD_DIM), vw.reshape(WINDOW, HEAD_DIM))


def scatter_kernel(
    att, dq, own, side, att_out, dq_out, dk_out, dv_out, halo, total, send, recv, hsend, hrecv
):
    x, z, core, y = place()
    my_slot = ((2 * z + core) % 4) * 4 + y
    head = z * 4 + y
    half = z // 2
    sibling = {"ctx": ctx_of(x, z, 1 - core), "head": y}
    beside = {"ctx": ctx_of(x_partner(x, core), z, 1 - core), "head": y}
    barrier = pltpu.get_barrier_semaphore()

    def greet(step, c):
        zz = (z + step // 4) % 4
        yy = (y + step % 4) % 4

        @pl.when((step > 0) | (half != core))
        def _():
            pl.semaphore_signal(
                barrier, inc=1, device_id={"ctx": ctx_of(x, zz, half), "head": yy}, device_id_type=MESH
            )

        return c

    lax.fori_loop(0, PIECES, greet, 0)
    pl.semaphore_signal(barrier, inc=1, device_id=sibling, device_id_type=MESH)
    pl.semaphore_signal(barrier, inc=1, device_id=beside, device_id_type=MESH)
    pl.semaphore_wait(barrier, jnp.where(half == core, PIECES - 1, PIECES) + 2)

    halos = []
    for a in range(2):
        halos.append(
            pltpu.make_async_remote_copy(
                src_ref=side.at[a, core],
                dst_ref=halo.at[a, 1],
                send_sem=hsend.at[a, 1],
                recv_sem=hrecv.at[a, 1],
                device_id=beside,
                device_id_type=MESH,
            )
        )
        halos.append(
            pltpu.make_async_remote_copy(
                src_ref=side.at[a, 1 - core],
                dst_ref=halo.at[a, 0],
                send_sem=hsend.at[a, 0],
                recv_sem=hrecv.at[a, 0],
                device_id=sibling,
                device_id_type=MESH,
            )
        )
    for copy in halos:
        copy.start()

    outs = (att_out, dq_out, dk_out, dv_out)
    srcs = (att, dq, total.at[0], total.at[1])

    def columns(h):
        return pl.ds(pl.multiple_of(h * HEAD_DIM, HEAD_DIM), HEAD_DIM)

    def slot_of(step):
        return (my_slot + step) % PIECES

    def place_of(s):
        return 2 * core + s // 8, (s // 4) % 2, s % 4

    def local(s):
        zz, cc, yy = place_of(s)
        return (zz == z) & (cc == core) & (yy == y)

    def piece(a, s):
        return srcs[a].at[pl.ds(pl.multiple_of(s * PIECE, PIECE), PIECE), :]

    def remote_copy(a, s):
        zz, cc, yy = place_of(s)
        return pltpu.make_async_remote_copy(
            src_ref=piece(a, s),
            dst_ref=outs[a].at[:, columns(head)],
            send_sem=send.at[a, s],
            recv_sem=recv.at[a, head],
            device_id={"ctx": ctx_of(x, zz, cc), "head": yy},
            device_id_type=MESH,
        )

    def send_all(a):
        def start(step, c):
            s = slot_of(step)
            mine = local(s)

            @pl.when(mine)
            def _():
                pltpu.make_async_copy(
                    piece(a, s), outs[a].at[:, columns(head)], recv.at[a, head]
                ).start()

            @pl.when(jnp.logical_not(mine))
            def _():
                remote_copy(a, s).start()

            return c

        lax.fori_loop(0, PIECES, start, 0)

    send_all(0)
    send_all(1)
    for a in range(2):
        halos[2 * a].wait_recv()
        halos[2 * a + 1].wait_recv()

        def sum_piece(s, c):
            cols = pl.ds(pl.multiple_of(s * PIECE, PIECE), PIECE)
            tot = (
                own[a, :, cols]
                + halo[a, 0, :, cols].astype(F32)
                + halo[a, 1, :, cols].astype(F32)
            )
            total[a, cols, :] = tot.T.astype(BF)
            return c

        lax.fori_loop(0, PIECES, sum_piece, 0)
        send_all(2 + a)
    for copy in halos:
        copy.wait_send()
    for a in range(4):

        def wait(h, c):
            part = outs[a].at[:, columns(h)]
            pltpu.make_async_copy(part, part, recv.at[a, h]).wait()

            @pl.when(jnp.logical_not(local(h)))
            def _():
                remote_copy(a, h).wait_send()

            return c

        lax.fori_loop(0, PIECES, wait, 0)


def scatter(att, dq, own, side):
    any_spec = pl.BlockSpec(memory_space=pl.ANY)
    out = jax.ShapeDtypeStruct((PIECE, PIECES * HEAD_DIM), BF)
    return pl.pallas_call(
        scatter_kernel,
        out_shape=(out,) * 4,
        in_specs=[any_spec, any_spec, pl.BlockSpec(memory_space=pltpu.VMEM), any_spec],
        out_specs=(any_spec,) * 4,
        scratch_shapes=[
            pltpu.VMEM((2, 2, HEAD_DIM, GROUP), BF),
            pltpu.VMEM((2, GROUP, HEAD_DIM), BF),
            pltpu.SemaphoreType.DMA((4, PIECES)),
            pltpu.SemaphoreType.DMA((4, PIECES)),
            pltpu.SemaphoreType.DMA((2, 2)),
            pltpu.SemaphoreType.DMA((2, 2)),
        ],
        compiler_params=pltpu.CompilerParams(
            collective_id=1, has_side_effects=True, vmem_limit_bytes=32 * 1024 * 1024
        ),
        name="to_tokens",
    )(att, dq, own, side)


def body(queries, keys_in, values, out_grad, doc_lengths):
    q, g, kw, vw = gather(queries, keys_in, values, out_grad)
    att, dq, own, side = attend(doc_lengths, q, g, kw, vw)
    return scatter(att, dq, own, side)


def solution(mesh):
    tokens = P(("ctx", "head"), None)
    return jax.shard_map(
        body,
        mesh=mesh,
        in_specs=(tokens,) * 4 + (P(),),
        out_specs=(tokens,) * 4,
        check_vma=False,
    )
```

profile of v0, /device:TPU:1, one launch (start us, length us, event | category | flops | bytes accessed | tf_op | source)
XLA Modules:
  0.0 128.6 jit_solution(182162339556512373)
XLA Ops:
  0.6 34.1 %to_heads.1 = (bf16[2048,128]{1,0:T(8,128)(2,1)}, bf16[2048,128]{1,0:T(8,128)(2,1)}, bf16[3,2048,128]{2,1,0:T(8,128)(2,1)}, bf16[3,2048,128]{2,1,0:T(8,128)(2,1)}) custom-call(bf16[128,2048]{1,0:T(8,128)(2,1)} %q_in.1, bf16[128,2048]{1,0:T(8,128)(2,1)} %k_in.1, bf16[128,2048]{1,0:T(8,128)(2,1)} %v_in.1, bf16[128,2048]{1,0:T(8,128)(2,1)} %g_in.1), custom_call_target="tpu_custom_call" | custom-call | tf_op jit(solution)/shard_map/to_heads/pallas_call | solution.py:171
  34.8 53.1 %attend.1 = (bf16[2048,128]{1,0:T(8,128)(2,1)}, bf16[2048,128]{1,0:T(8,128)(2,1)}, f32[2,128,2048]{2,1,0:T(8,128)}, bf16[2,2,128,2048]{3,2,1,0:T(8,128)(2,1)}) custom-call(s32[15]{0:T(128)} %lens.1, bf16[2048,128]{1,0:T(8,128)(2,1)} %get-tuple-element.12.q_ref, bf16[2048,128]{1,0:T(8,128)(2,1)} %get-tuple-element.13.g_ref, bf16[6144,128]{1,0:T(8,128)(2,1)} %bitcast.2, ...), custom_call_target="tpu_custom_call" | custom-call | tf_op jit(solution)/shard_map/attend/pallas_call | solution.py:315
  87.9 0.0 copy-start
  87.9 1.6 %copy-done = f32[2,128,2048]{2,1,0:T(8,128)S(1)} copy-done((f32[2,128,2048]{2,1,0:T(8,128)S(1)}, f32[2,128,2048]{2,1,0:T(8,128)}, u32[]{:S(2)}) %copy-start) | copy-done | bytes 2097176
  89.5 0.0 copy-start.1
  89.5 1.6 %copy-done.1 = bf16[2,2,128,2048]{3,2,1,0:T(8,128)(2,1)S(1)} copy-done((bf16[2,2,128,2048]{3,2,1,0:T(8,128)(2,1)S(1)}, bf16[2,2,128,2048]{3,2,1,0:T(8,128)(2,1)}, u32[]{:S(2)}) %copy-start.1) | copy-done | bytes 2097176
  91.1 0.0 copy-start.2
  91.1 1.0 copy-done.2
  92.1 0.0 copy-start.3
  92.1 1.0 copy-done.3
  93.2 32.2 %to_tokens.1 = (bf16[128,2048]{1,0:T(8,128)(2,1)S(1)}, bf16[128,2048]{1,0:T(8,128)(2,1)S(1)}, bf16[128,2048]{1,0:T(8,128)(2,1)S(1)}, bf16[128,2048]{1,0:T(8,128)(2,1)S(1)}) custom-call(bf16[2048,128]{1,0:T(8,128)(2,1)S(1)} %copy-done.2, bf16[2048,128]{1,0:T(8,128)(2,1)S(1)} %copy-done.3, f32[2,128,2048]{2,1,0:T(8,128)S(1)} %copy-done, ...), custom_call_target="tpu_custom_call" | custom-call | tf_op jit(solution)/shard_map/to_tokens/pallas_call | solution.py:480
  125.4 0.8 copy.13
  126.2 0.8 copy.14
  127.0 0.8 copy.15
  127.8 0.8 copy.16
Async XLA Ops:
  87.9 1.6 %copy-start = (f32[2,128,2048]{2,1,0:T(8,128)S(1)}, f32[2,128,2048]{2,1,0:T(8,128)}, u32[]{:S(2)}) copy-start(f32[2,128,2048]{2,1,0:T(8,128)} %get-tuple-element.18.own) | copy-start | bytes 6291460
  89.5 1.6 %copy-start.1 = (bf16[2,2,128,2048]{3,2,1,0:T(8,128)(2,1)S(1)}, bf16[2,2,128,2048]{3,2,1,0:T(8,128)(2,1)}, u32[]{:S(2)}) copy-start(bf16[2,2,128,2048]{3,2,1,0:T(8,128)(2,1)} %get-tuple-element.19.side) | copy-start | bytes 6291460
  91.1 1.0 copy-start.2
  92.1 1.0 copy-start.3
where the time goes:
time: 129 us
  Pallas kernels  119 us (92%)
  local copies, waits for them, and re-layouts  8.44 us (7%)
    pallas_call x1, Pallas kernels, attend(): pl.pallas_call(attend_kernel, out_shape=(own, own, jax.ShapeDtypeStruct((...  53.1 us
    pallas_call x1, Pallas kernels, gather(): pl.pallas_call(gather_kernel, out_shape=(own, own, window, window), in_sp...  34.1 us
    pallas_call x1, Pallas kernels, scatter(): pl.pallas_call(scatter_kernel, out_shape=(out,) * 4, in_specs=[any_spec,...  32.2 us
    unnamed x12, local copies, waits for them, and re-layouts  8.44 us

commit v1 on v0

--- a/solution.py
+++ b/solution.py
@@ -13,11 +13,11 @@
 PIECE = 128
 PIECES = GROUP // PIECE
 QT = 256
-KT = 512
-UNIT = 256
+KT = 2304
+UNIT = 128
 WINDOW = 3 * GROUP
-PADDED = WINDOW + KT
-SPAN = 9 * KT
+BT = 256
+STEPS = -(-(2 * GROUP + QT + UNIT) // KT)
 TOKENS = 16384
 MASK = 1024.0
 SCALE = HEAD_DIM ** (-0.5)
@@ -209,27 +209,21 @@
         ends = jnp.where(lane == j, bounds[-1], ends)
     starts = jnp.where(lane == 127, TOKENS, jnp.where(lane == 126, -(1 << 30), starts))
     ends = jnp.where(lane == 126, 0, ends)
-    row = lax.broadcasted_iota(jnp.int32, (QT, 128), 0)
-
-    def in_doc(first):
-        pos = first + row
+
+    def in_doc(first, count):
+        pos = first + lax.broadcasted_iota(jnp.int32, (count, 128), 0)
         return (pos >= starts) & (pos < ends)
 
-    ones = jnp.ones((QT, 128), BF)
+    ones = jnp.ones((BT, 128), BF)
 
     def build(b, c):
-        rows = pl.ds(pl.multiple_of(b * QT, QT), QT)
-        flag = jnp.where(in_doc(base + b * QT), -MASK, 0.0).astype(BF)
+        rows = pl.ds(pl.multiple_of(b * BT, BT), BT)
+        flag = jnp.where(in_doc(base + b * BT, BT), -MASK, 0.0).astype(BF)
         ke[rows, :] = jnp.concatenate([kw[rows, :], flag], axis=1)
         ve[rows, :] = jnp.concatenate([vw[rows, :], ones], axis=1)
         return c
 
-    lax.fori_loop(0, WINDOW // QT, build, 0)
-    for b in range(WINDOW // QT, PADDED // QT):
-        rows = pl.ds(b * QT, QT)
-        flag = jnp.where(in_doc(base + b * QT), -MASK, 0.0).astype(BF)
-        ke[rows, :] = jnp.concatenate([jnp.zeros((QT, 128), BF), flag], axis=1)
-        ve[rows, :] = jnp.zeros((QT, 256), BF)
+    lax.fori_loop(0, WINDOW // BT, build, 0)
     dk_acc[...] = jnp.zeros_like(dk_acc)
     dv_acc[...] = jnp.zeros_like(dv_acc)
 
@@ -245,19 +239,21 @@
             hi = jnp.where(e > r0 + (QT - 1), jnp.minimum(hi, e), hi)
         first = (lo - base) // UNIT
         steps = (hi - base - first * UNIT + (KT - 1)) // KT
+        first = jnp.minimum(first, (WINDOW - steps * KT) // UNIT)
 
         q = q_ref[rows, :]
         g = g_ref[rows, :]
-        qe = jnp.concatenate([q, jnp.where(in_doc(r0), 0.0, MASK).astype(BF)], axis=1)
-
-        def krows(t):
-            return pl.ds(pl.multiple_of(first * UNIT + t * KT, UNIT), KT)
+        qe = jnp.concatenate([q, jnp.where(in_doc(r0, QT), 0.0, MASK).astype(BF)], axis=1)
+
+        def krows(t, j=0, n=KT):
+            return pl.ds(pl.multiple_of(first * UNIT + t * KT + j, UNIT), n)
 
         def score_step(t, peak):
-            s = dot_nt(qe, ke[krows(t), :])
-            s_scr[t] = s
-            for j in range(KT // 128):
-                peak = jnp.maximum(peak, s[:, j * 128:(j + 1) * 128])
+            for o in range(0, KT, KT):
+                s = dot_nt(qe, ke[krows(t, o, KT), :])
+                s_scr[t, :, o:o + KT] = s
+                for j in range(KT // 128):
+                    peak = jnp.maximum(peak, s[:, j * 128:(j + 1) * 128])
             return peak
 
         peak = lax.fori_loop(0, steps, score_step, jnp.full((QT, 128), -3e38, F32))
@@ -266,9 +262,12 @@
         o_acc[...] = jnp.zeros_like(o_acc)
 
         def prob_step(t, c):
-            p = jnp.exp2((s_scr[t] - peak) * (SCALE * LOG2E)).astype(BF)
-            p_scr[t] = p
-            o_acc[...] += dot_nn(p, ve[krows(t), :])
+            tot = o_acc[...]
+            for o in range(0, KT, KT):
+                p = jnp.exp2((s_scr[t, :, o:o + KT] - peak) * (SCALE * LOG2E)).astype(BF)
+                p_scr[t, :, o:o + KT] = p
+                tot += dot_nn(p, ve[krows(t, o, KT), :])
+            o_acc[...] = tot
             return c
 
         lax.fori_loop(0, steps, prob_step, 0)
@@ -289,13 +288,16 @@
         dq_acc[...] = jnp.zeros_like(dq_acc)
 
         def grad_step(t, c):
-            keys = krows(t)
-            p = p_scr[t]
-            dp = dot_nt(ge, ve[keys, :])
-            ds = (p.astype(F32) * dp).astype(BF)
-            dq_acc[...] += dot_nn(ds, ke[keys, :128])
-            dk_acc[:, keys] += dot_nn(qt, ds)
-            dv_acc[:, keys] += dot_nn(gt, p)
+            tot = dq_acc[...]
+            for o in range(0, KT, KT):
+                keys = krows(t, o, KT)
+                p = p_scr[t, :, o:o + KT]
+                dp = dot_nt(ge, ve[keys, :])
+                ds = (p.astype(F32) * dp).astype(BF)
+                tot += dot_nn(ds, ke[keys, :128])
+                dk_acc[:, keys] += dot_nn(qt, ds)
+                dv_acc[:, keys] += dot_nn(gt, p)
+            dq_acc[...] = tot
             return c
 
         lax.fori_loop(0, steps, grad_step, 0)
@@ -323,14 +325,14 @@
         in_specs=[pl.BlockSpec(memory_space=pltpu.SMEM)] + [vmem] * 4,
         out_specs=(vmem,) * 4,
         scratch_shapes=[
-            pltpu.VMEM((PADDED, 256), BF),
-            pltpu.VMEM((PADDED, 256), BF),
-            pltpu.VMEM((SPAN // KT, QT, KT), F32),
-            pltpu.VMEM((SPAN // KT, QT, KT), BF),
+            pltpu.VMEM((WINDOW, 256), BF),
+            pltpu.VMEM((WINDOW, 256), BF),
+            pltpu.VMEM((STEPS, QT, KT), F32),
+            pltpu.VMEM((STEPS, QT, KT), BF),
             pltpu.VMEM((QT, 256), F32),
             pltpu.VMEM((QT, 128), F32),
-            pltpu.VMEM((128, PADDED), F32),
-            pltpu.VMEM((128, PADDED), F32),
+            pltpu.VMEM((128, WINDOW), F32),
+            pltpu.VMEM((128, WINDOW), F32),
         ],
         compiler_params=pltpu.CompilerParams(vmem_limit_bytes=56 * 1024 * 1024),
         name="attend",
@@ -480,7 +482,7 @@
     return pl.pallas_call(
         scatter_kernel,
         out_shape=(out,) * 4,
-        in_specs=[any_spec, any_spec, pl.BlockSpec(memory_space=pltpu.VMEM), any_spec],
+        in_specs=[pl.BlockSpec(memory_space=pltpu.VMEM)] * 4,
         out_specs=(any_spec,) * 4,
         scratch_shapes=[
             pltpu.VMEM((2, 2, HEAD_DIM, GROUP), BF),

time: 129 us -> 104 us (0.81); the launches traced: 129 us -> 102 us
  Pallas kernels: 119 us -> 92.8 us
    pallas_call x1, Pallas kernels: 53.1 us -> 28.5 us  [attend(): pl.pallas_call(attend_kernel, out_shape=(own, own, jax.ShapeDtypeStruct((...]
    pallas_call x1, Pallas kernels: 32.2 us -> 30.2 us  [scatter(): pl.pallas_call(scatter_kernel, out_shape=(out,) * 4, in_specs=[pl.BlockSp...]
where the time goes in v1:
time: 104 us; the launch traced here: 102 us
  Pallas kernels  92.8 us (89%)
  local copies, waits for them, and re-layouts  8.44 us (8%)
    pallas_call x1, Pallas kernels, gather(): pl.pallas_call(gather_kernel, out_shape=(own, own, window, window), in_sp...  34.1 us
    pallas_call x1, Pallas kernels, scatter(): pl.pallas_call(scatter_kernel, out_shape=(out,) * 4, in_specs=[pl.BlockSp...  30.2 us
    pallas_call x1, Pallas kernels, attend(): pl.pallas_call(attend_kernel, out_shape=(own, own, jax.ShapeDtypeStruct((...  28.5 us
    unnamed x12, local copies, waits for them, and re-layouts  8.44 us

profile of v1, /device:TPU:1, one launch (start us, length us, event | category | flops | bytes accessed | tf_op | source)
XLA Modules:
  0.0 101.9 jit_solution(7500859043474564832)
XLA Ops:
  0.6 34.1 %to_heads.1 = (bf16[2048,128]{1,0:T(8,128)(2,1)}, bf16[2048,128]{1,0:T(8,128)(2,1)}, bf16[3,2048,128]{2,1,0:T(8,128)(2,1)}, bf16[3,2048,128]{2,1,0:T(8,128)(2,1)}) custom-call(bf16[128,2048]{1,0:T(8,128)(2,1)} %q_in.1, bf16[128,2048]{1,0:T(8,128)(2,1)} %k_in.1, bf16[128,2048]{1,0:T(8,128)(2,1)} %v_in.1, bf16[128,2048]{1,0:T(8,128)(2,1)} %g_in.1), custom_call_target="tpu_custom_call" | custom-call | tf_op jit(solution)/shard_map/to_heads/pallas_call | solution.py:171
  34.8 28.5 %attend.1 = (bf16[2048,128]{1,0:T(8,128)(2,1)}, bf16[2048,128]{1,0:T(8,128)(2,1)}, f32[2,128,2048]{2,1,0:T(8,128)}, bf16[2,2,128,2048]{3,2,1,0:T(8,128)(2,1)}) custom-call(s32[15]{0:T(128)} %lens.1, bf16[2048,128]{1,0:T(8,128)(2,1)} %get-tuple-element.12.q_ref, bf16[2048,128]{1,0:T(8,128)(2,1)} %get-tuple-element.13.g_ref, bf16[6144,128]{1,0:T(8,128)(2,1)} %bitcast.2, ...), custom_call_target="tpu_custom_call" | custom-call | tf_op jit(solution)/shard_map/attend/pallas_call | solution.py:317
  63.3 0.0 copy-start
  63.3 1.6 %copy-done = f32[2,128,2048]{2,1,0:T(8,128)S(1)} copy-done((f32[2,128,2048]{2,1,0:T(8,128)S(1)}, f32[2,128,2048]{2,1,0:T(8,128)}, u32[]{:S(2)}) %copy-start) | copy-done | bytes 2097176
  64.9 0.0 copy-start.1
  64.9 1.6 %copy-done.1 = bf16[2,2,128,2048]{3,2,1,0:T(8,128)(2,1)S(1)} copy-done((bf16[2,2,128,2048]{3,2,1,0:T(8,128)(2,1)S(1)}, bf16[2,2,128,2048]{3,2,1,0:T(8,128)(2,1)}, u32[]{:S(2)}) %copy-start.1) | copy-done | bytes 2097176
  66.4 0.0 copy-start.2
  66.4 1.0 %copy-done.2 = bf16[2048,128]{1,0:T(8,128)(2,1)S(1)} copy-done((bf16[2048,128]{1,0:T(8,128)(2,1)S(1)}, bf16[2048,128]{1,0:T(8,128)(2,1)}, u32[]{:S(2)}) %copy-start.2) | copy-done | bytes 524312
  67.5 0.0 copy-start.3
  67.5 1.0 %copy-done.3 = bf16[2048,128]{1,0:T(8,128)(2,1)S(1)} copy-done((bf16[2048,128]{1,0:T(8,128)(2,1)S(1)}, bf16[2048,128]{1,0:T(8,128)(2,1)}, u32[]{:S(2)}) %copy-start.3) | copy-done | bytes 524312
  68.5 30.2 %to_tokens.1 = (bf16[128,2048]{1,0:T(8,128)(2,1)S(1)}, bf16[128,2048]{1,0:T(8,128)(2,1)S(1)}, bf16[128,2048]{1,0:T(8,128)(2,1)S(1)}, bf16[128,2048]{1,0:T(8,128)(2,1)S(1)}) custom-call(bf16[2048,128]{1,0:T(8,128)(2,1)S(1)} %copy-done.2, bf16[2048,128]{1,0:T(8,128)(2,1)S(1)} %copy-done.3, f32[2,128,2048]{2,1,0:T(8,128)S(1)} %copy-done, ...), custom_call_target="tpu_custom_call" | custom-call | tf_op jit(solution)/shard_map/to_tokens/pallas_call | solution.py:482
  98.8 0.8 copy.13
  99.5 0.8 copy.14
  100.3 0.8 copy.15
  101.1 0.8 copy.16
Async XLA Ops:
  63.3 1.6 %copy-start = (f32[2,128,2048]{2,1,0:T(8,128)S(1)}, f32[2,128,2048]{2,1,0:T(8,128)}, u32[]{:S(2)}) copy-start(f32[2,128,2048]{2,1,0:T(8,128)} %get-tuple-element.18.own) | copy-start | bytes 6291460
  64.9 1.6 %copy-start.1 = (bf16[2,2,128,2048]{3,2,1,0:T(8,128)(2,1)S(1)}, bf16[2,2,128,2048]{3,2,1,0:T(8,128)(2,1)}, u32[]{:S(2)}) copy-start(bf16[2,2,128,2048]{3,2,1,0:T(8,128)(2,1)} %get-tuple-element.19.side) | copy-start | bytes 6291460
  66.4 1.0 %copy-start.2 = (bf16[2048,128]{1,0:T(8,128)(2,1)S(1)}, bf16[2048,128]{1,0:T(8,128)(2,1)}, u32[]{:S(2)}) copy-start(bf16[2048,128]{1,0:T(8,128)(2,1)} %get-tuple-element.16.att) | copy-start | bytes 1572868
  67.5 1.0 %copy-start.3 = (bf16[2048,128]{1,0:T(8,128)(2,1)S(1)}, bf16[2048,128]{1,0:T(8,128)(2,1)}, u32[]{:S(2)}) copy-start(bf16[2048,128]{1,0:T(8,128)(2,1)} %get-tuple-element.17.dq) | copy-start | bytes 1572868
